TPU v7x, 32 devices: a whole 2x2x4 slice. The times are simulated.
32 devices in a mesh: member: 2 (over y), row: 4 (over z), col: 4 (over x, core).
Axes of the slice: x: 2, y: 2, z: 4, core: 2. Of those that a mesh axis runs over, the one named last changes fastest.
Arguments:
- tokens: bfloat16 [128, 8192], P(('member', 'row'), 'col'), parts along dimension 0, may hold values from -6 to 6
- output_grad: bfloat16 [128, 8192], P(('member', 'row'), 'col'), parts along dimension 0, may hold values from -6 to 6
- gate_weight: bfloat16 [32768, 8192], P(('member', 'row'), 'col'), parts along dimension 0, may hold values from -0.09375 to 0.09375
- up_weight: bfloat16 [32768, 8192], P(('member', 'row'), 'col'), parts along dimension 0, may hold values from -0.09375 to 0.09375
- down_weight: bfloat16 [16384, 16384], P(('member', 'col'), 'row'), parts along dimension 0, may hold values from -0.0625 to 0.0625
- gate_mask: int32 [128, 64], P('row', 'col'), may hold values from 0 to 1, as said below
- up_mask: int32 [128, 64], P('row', 'col'), may hold values from 0 to 1, as said below
- down_mask: int32 [64, 128], P('col', 'row'), may hold values from 0 to 1, as said below
Outputs:
- output: bfloat16 [128, 8192], P(('member', 'row'), 'col'), parts along dimension 0
- input_grad: bfloat16 [128, 8192], P(('member', 'row'), 'col'), parts along dimension 0
- gate_grad: bfloat16 [32768, 8192], P(('member', 'row'), 'col'), parts along dimension 0
- up_grad: bfloat16 [32768, 8192], P(('member', 'row'), 'col'), parts along dimension 0
- down_grad: bfloat16 [16384, 16384], P(('member', 'col'), 'row'), parts along dimension 0
There are 2 independent parts, one for each index of `member`. A program takes and returns all parts, laid end to end along the dimension named above; an argument that names none is the same for every part. Nothing has to cross between parts.
Inputs may be any that keep to these rules, and one draw needn't show every extreme that they name: `gate_mask`: each entry is 0 (block pruned) or 1 (block kept); the share of kept blocks differs between regions of the matrix. `up_mask`: each entry is 0 (block pruned) or 1 (block kept); the share of kept blocks differs between regions of the matrix. `down_mask`: each entry is 0 (block pruned) or 1 (block kept); the share of kept blocks differs between regions of the matrix.
All inputs are finite; a program needn't handle non-finite values.
Results may differ from a plain program's by a relative error of at most 0.017.
Values may be sent and summed in bfloat16 or wider, within the bound.
No kernel may reach another device: no remote copies, remote signals or barrier semaphores. Data moves between devices by JAX's collectives and lax.ppermute only.
A program may use at most 320 MiB of HBM per device.

v0:
```python
import functools

import jax
import jax.numpy as jnp
from jax import lax
from jax.experimental import pallas as pl
from jax.experimental.pallas import tpu as pltpu
from jax.sharding import PartitionSpec as P

B16 = jnp.bfloat16
F32 = jnp.float32
BLOCK = 128
MIB = 2**20
OWN, FAR = 0, 1
CUTS = 1

VMEM = pl.BlockSpec(memory_space=pltpu.VMEM)
SMEM = pl.BlockSpec(memory_space=pltpu.SMEM)
ANY = pl.BlockSpec(memory_space=pl.ANY)


def contract(left, right, left_dim, right_dim):
    return lax.dot_general(
        left, right, (((left_dim,), (right_dim,)), ((), ())), preferred_element_type=F32
    )


def keep_blocks(tile, kept):
    rows = []
    for i in range(tile.shape[0] // BLOCK):
        row = []
        for j in range(tile.shape[1] // BLOCK):
            block = tile[BLOCK * i : BLOCK * (i + 1), BLOCK * j : BLOCK * (j + 1)]
            row.append(jnp.where(kept(i, j) != 0, block, jnp.zeros_like(block)))
        rows.append(row[0] if len(row) == 1 else jnp.concatenate(row, 1))
    return rows[0] if len(rows) == 1 else jnp.concatenate(rows, 0)


def stacked(refs, rows, span):
    parts = [ref[rows, span] for ref in refs]
    return parts[0] if len(parts) == 1 else jnp.concatenate(parts, 0)


def half_of_pair(side):
    return (lax.axis_index("col") + side) % 2


def total(parts):
    return functools.reduce(lambda a, b: a + b, parts)


def fit(size, most):
    return size if size < most else most


def params(mib):
    return pltpu.CompilerParams(vmem_limit_bytes=mib * MIB)


def cost(flops, read):
    return pl.CostEstimate(flops=flops, bytes_accessed=read, transcendentals=0)


def resident(arrays):
    return [pltpu.with_memory_space_constraint(a, pltpu.VMEM) for a in arrays]


def piece_shapes(weight, dim, pieces):
    shape = list(weight.shape)
    shape[dim] //= 2 * pieces
    return [tuple(shape)] * pieces


def piece_copies(source_ref, dim, side, out_refs, sems):
    copies = []
    for p, out_ref in enumerate(out_refs):
        height, size = out_ref.shape[0] // CUTS, out_ref.shape[dim]
        first = pl.multiple_of((half_of_pair(side) * len(out_refs) + p) * size, BLOCK)
        for cut in range(CUTS):
            here = pl.ds(cut * height, height)
            if dim == 0:
                source = source_ref.at[pl.ds(first + cut * height, height)]
            else:
                source = source_ref.at[here, pl.ds(first, size)]
            copies.append(
                pltpu.make_async_copy(source, out_ref.at[here], sems.at[p * CUTS + cut])
            )
    return copies


def join(top, bottom):
    height, width = top.shape

    def kernel(top_ref, bottom_ref, out_ref, sems):
        copies = [
            pltpu.make_async_copy(ref, out_ref.at[pl.ds(n * height, height)], sems.at[n])
            for n, ref in enumerate((top_ref, bottom_ref))
        ]
        for copy in copies:
            copy.start()
        for copy in copies:
            copy.wait()

    return pl.pallas_call(
        kernel,
        name="join",
        in_specs=[ANY] * 2,
        out_specs=VMEM,
        out_shape=jax.ShapeDtypeStruct((2 * height, width), top.dtype),
        scratch_shapes=[pltpu.SemaphoreType.DMA((2,))],
        compiler_params=params(1),
    )(in_hbm(top), in_hbm(bottom))


def in_hbm(array):
    return pltpu.with_memory_space_constraint(array, pltpu.HBM)


def load(items, pieces):
    count = len(items)
    shapes = [s for weight, dim in items for s in piece_shapes(weight, dim, pieces) * 2]

    def kernel(*refs):
        outs, sems = refs[count:-1], refs[-1]
        copies = []
        for n, (_, dim) in enumerate(items):
            for side in (OWN, FAR):
                at = (2 * n + side) * pieces
                copies += piece_copies(
                    refs[n], dim, side, outs[at : at + pieces],
                    sems.at[pl.ds(at * CUTS, pieces * CUTS)],
                )
        for copy in copies:
            copy.start()
        for copy in copies:
            copy.wait()

    loaded = pl.pallas_call(
        kernel,
        name="load",
        in_specs=[ANY] * count,
        out_specs=[VMEM] * len(shapes),
        out_shape=[pltpu.VMEM(s, B16) for s in shapes],
        scratch_shapes=[pltpu.SemaphoreType.DMA((len(shapes) * CUTS,))],
        compiler_params=params(1),
        cost_estimate=cost(0, sum(w.size * 2 for w, _ in items)),
    )(*[in_hbm(w) for w, _ in items])
    return [
        [loaded[(2 * n + side) * pieces : (2 * n + side + 1) * pieces] for side in (OWN, FAR)]
        for n in range(count)
    ]


def down_forward(side, mask, weight, grads, recv=None, after=()):
    pieces, parts = len(weight), len(grads)
    rows, depth = grads[0].shape[0] // 2, grads[0].shape[1]
    tokens = parts * rows
    width = weight[0].shape[1]
    tile = fit(width, 1024)
    step = fit(depth, 256)

    def kernel(mask_ref, *rest):
        weight_refs, grads_refs = rest[:pieces], rest[pieces : pieces + parts]
        recv_ref, out_ref = rest[pieces + parts], rest[-1]
        for p in range(pieces):
            base = (half_of_pair(side) * pieces + p) * (width // BLOCK)

            def one(t, carry):
                start = pl.multiple_of(t * tile, BLOCK)
                here = pl.ds(pl.multiple_of(p * width + t * tile, BLOCK), tile)
                acc = total(
                    contract(
                        stacked(grads_refs, slice(rows, None), slice(k, k + step)),
                        keep_blocks(
                            weight_refs[p][k : k + step, pl.ds(start, tile)],
                            lambda i, j: mask_ref[k // BLOCK + i, base + start // BLOCK + j],
                        ),
                        1,
                        0,
                    )
                    for k in range(0, depth, step)
                )
                if recv is not None:
                    acc = acc + recv_ref[:, here].astype(F32)
                out_ref[:, here] = acc.astype(B16)
                return carry

            lax.fori_loop(0, width // tile, one, 0)

    more = [] if recv is None else [recv]
    return pl.pallas_call(
        kernel,
        name="down_forward",
        in_specs=[SMEM] + [VMEM] * (pieces + parts + len(more)) + [ANY] * len(after),
        out_specs=VMEM,
        out_shape=jax.ShapeDtypeStruct((tokens, pieces * width), B16),
        compiler_params=params(4),
        cost_estimate=cost(1, 1),
    )(mask, *resident(weight), *grads, *more, *after)


def up_forward(side, mask, weight, tokens, recv=None, after=()):
    pieces, parts = len(weight), len(tokens)
    rows, depth = tokens[0].shape[0] // 2, tokens[0].shape[1]
    count = parts * rows
    width = weight[0].shape[0]
    tile = fit(width // 2, 512)
    step = fit(depth, 256)

    def kernel(mask_ref, *rest):
        weight_refs, tokens_refs = rest[:pieces], rest[pieces : pieces + parts]
        recv_ref, out_ref = rest[pieces + parts], rest[-1]
        for p in range(pieces):
            base = (half_of_pair(side) * pieces + p) * (width // BLOCK)

            def one(t, carry):
                starts = [pl.multiple_of((2 * t + n) * tile, BLOCK) for n in range(2)]
                both = jnp.concatenate(
                    [
                        total(
                            contract(
                                keep_blocks(
                                    weight_refs[p][pl.ds(start, tile), k : k + step],
                                    lambda i, j: mask_ref[k // BLOCK + j, base + start // BLOCK + i],
                                ),
                                stacked(tokens_refs, slice(0, rows), slice(k, k + step)),
                                1,
                                1,
                            )
                            for k in range(0, depth, step)
                        )
                        for start in starts
                    ],
                    1,
                ).T
                for n in range(2):
                    here = pl.ds(pl.multiple_of(p * width + (2 * t + n) * tile, BLOCK), tile)
                    out = both[n * count : (n + 1) * count]
                    if recv is not None:
                        out = out + recv_ref[:, here].astype(F32)
                    out_ref[:, here] = out.astype(B16)
                return carry

            lax.fori_loop(0, width // (2 * tile), one, 0)

    more = [] if recv is None else [recv]
    return pl.pallas_call(
        kernel,
        name="up_forward",
        in_specs=[SMEM] + [VMEM] * (pieces + parts + len(more)) + [ANY] * len(after),
        out_specs=VMEM,
        out_shape=jax.ShapeDtypeStruct((count, pieces * width), B16),
        compiler_params=params(4),
        cost_estimate=cost(1, 1),
    )(mask.T, *resident(weight), *tokens, *more, *after)


def activate(gate, gate_far, up, up_far):
    def kernel(gate_ref, gate_far_ref, up_ref, up_far_ref, out_ref):
        gate_sum = gate_ref[...].astype(F32) + gate_far_ref[...].astype(F32)
        up_sum = up_ref[...].astype(F32) + up_far_ref[...].astype(F32)
        out_ref[...] = (gate_sum * jax.nn.sigmoid(gate_sum) * up_sum).astype(B16)

    return pl.pallas_call(
        kernel,
        name="activate",
        in_specs=[VMEM] * 4,
        out_specs=VMEM,
        out_shape=jax.ShapeDtypeStruct(gate.shape, B16),
        compiler_params=params(4),
        cost_estimate=cost(gate.size * 300, 0),
    )(gate, gate_far, up, up_far)


def deltas(gate, gate_far, up, up_far, delta, delta_far, after=()):
    count, width = gate.shape

    def kernel(gate_ref, gate_far_ref, up_ref, up_far_ref, delta_ref, delta_far_ref, *rest):
        out_ref = rest[-1]
        gate_sum = gate_ref[...].astype(F32) + gate_far_ref[...].astype(F32)
        up_sum = up_ref[...].astype(F32) + up_far_ref[...].astype(F32)
        hidden_delta = delta_ref[...].astype(F32) + delta_far_ref[...].astype(F32)
        sigmoid = jax.nn.sigmoid(gate_sum)
        out_ref[:count] = (
            hidden_delta * up_sum * sigmoid * (1.0 + gate_sum * (1.0 - sigmoid))
        ).astype(B16)
        out_ref[count:] = (hidden_delta * (gate_sum * sigmoid)).astype(B16)

    return pl.pallas_call(
        kernel,
        name="deltas",
        in_specs=[VMEM] * 6 + [ANY] * len(after),
        out_specs=VMEM,
        out_shape=jax.ShapeDtypeStruct((2 * count, width), B16),
        compiler_params=params(4),
        cost_estimate=cost(gate.size * 300, 0),
    )(gate, gate_far, up, up_far, delta, delta_far, *after)


def output_part(side, mask, weight, hidden, before=None, after=()):
    pieces = len(weight)
    count = hidden.shape[0]
    depth, width = weight[0].shape
    tile = fit(depth // 2, 512)
    step = fit(width, 256)

    def kernel(mask_ref, *rest):
        weight_refs, hidden_ref, before_ref, out_ref = rest[:pieces], rest[pieces], rest[pieces + 1], rest[-1]
        base = half_of_pair(side) * pieces * (width // BLOCK)

        def one(t, carry):
            starts = [pl.multiple_of((2 * t + n) * tile, BLOCK) for n in range(2)]
            both = jnp.concatenate(
                [
                    total(
                        contract(
                            keep_blocks(
                                weight_refs[p][pl.ds(start, tile), k : k + step],
                                lambda i, j: mask_ref[
                                    start // BLOCK + i, base + (p * width + k) // BLOCK + j
                                ],
                            ),
                            hidden_ref[:, p * width + k : p * width + k + step],
                            1,
                            1,
                        )
                        for p in range(pieces)
                        for k in range(0, width, step)
                    )
                    for start in starts
                ],
                1,
            ).T
            for n, start in enumerate(starts):
                out = both[n * count : (n + 1) * count]
                if before is not None:
                    out = out + before_ref[:, pl.ds(start, tile)]
                out_ref[:, pl.ds(start, tile)] = out
            return carry

        lax.fori_loop(0, depth // (2 * tile), one, 0)

    more = [] if before is None else [before]
    return pl.pallas_call(
        kernel,
        name="output_part",
        in_specs=[SMEM] + [VMEM] * (pieces + 1 + len(more)) + [ANY] * len(after),
        out_specs=VMEM,
        out_shape=jax.ShapeDtypeStruct((count, depth), F32),
        compiler_params=params(4),
        cost_estimate=cost(1, 1),
    )(mask, *resident(weight), hidden, *more, *after)


def input_part(side, masks, gate, up, delta, before=None, output=None, blocks=1):
    pieces = len(gate)
    count = delta.shape[0] // 2
    width, depth = gate[0].shape
    tile = fit(depth, 1024)
    step = fit(width, 256)
    rows = count // blocks

    def kernel(gate_mask_ref, up_mask_ref, *rest):
        gate_refs, up_refs, delta_ref = rest[:pieces], rest[pieces : 2 * pieces], rest[2 * pieces]
        rest = rest[2 * pieces + 1 :]
        base = half_of_pair(side) * pieces * (width // BLOCK)

        def one(t, carry):
            start = pl.multiple_of(t * tile, BLOCK)
            here = pl.ds(start, tile)
            acc = total(
                contract(
                    delta_ref[row : row + count, p * width + k : p * width + k + step],
                    keep_blocks(
                        refs[p][k : k + step, here],
                        lambda i, j: mask_ref[
                            start // BLOCK + j, base + (p * width + k) // BLOCK + i
                        ],
                    ),
                    1,
                    0,
                )
                for refs, mask_ref, row in (
                    (gate_refs, gate_mask_ref, 0),
                    (up_refs, up_mask_ref, count),
                )
                for p in range(pieces)
                for k in range(0, width, step)
            )
            if before is None:
                rest[0][:, here] = acc
            else:
                acc = (acc + rest[0][:, here]).astype(B16)
                out = rest[1][:, here].astype(B16)
                for b in range(blocks):
                    rest[2 + b][:rows, here] = out[b * rows : (b + 1) * rows]
                    rest[2 + b][rows:, here] = acc[b * rows : (b + 1) * rows]
            return carry

        lax.fori_loop(0, depth // tile, one, 0)

    if before is None:
        more, out_shape = [], [jax.ShapeDtypeStruct((count, depth), F32)]
    else:
        more = [before, output]
        out_shape = [jax.ShapeDtypeStruct((2 * rows, depth), B16)] * blocks
    return pl.pallas_call(
        kernel,
        name="input_part",
        in_specs=[SMEM] * 2 + [VMEM] * (2 * pieces + 1 + len(more)),
        out_specs=[VMEM] * len(out_shape),
        out_shape=out_shape,
        compiler_params=params(4),
        cost_estimate=cost(16 * count * depth * width * pieces, 0),
    )(masks[0].T, masks[1].T, *resident(gate), *resident(up), delta, *more)


def weight_grads(masks, joint, hidden, delta):
    parts = len(joint)
    rows, depth = joint[0].shape[0] // 2, joint[0].shape[1]
    count = parts * rows
    width = hidden[0].shape[1]
    tall = fit(width, 1024)
    wide = fit(min(width, depth), 2048)
    chunk = fit(wide, 512)
    slots = 3

    def kernel(gate_mask_ref, up_mask_ref, down_mask_ref, *rest):
        hidden_refs, delta_refs = rest[:2], rest[2:4]
        rest = rest[4:]
        joint_refs = rest[:parts]
        gate_out, up_out, down_out, ring, sems, hidden_all, turned, tokens_all, grads_turned = rest[parts:]
        for side in (OWN, FAR):
            hidden_all[side] = hidden_refs[side][...]
            for kind in range(2):
                turned[kind, side] = delta_refs[side][kind * count : (kind + 1) * count].T
        tokens_all[...] = stacked(joint_refs, slice(0, rows), slice(None))
        grads_turned[...] = stacked(joint_refs, slice(rows, None), slice(None)).T

        def copy(slot, target):
            return pltpu.make_async_copy(ring.at[slot], target, sems.at[slot])

        def tiles(done, out_ref, mask_ref, height, columns, row_tile, column_tile, left, right, place):
            across = columns // column_tile
            each = (height // row_tile) * across

            def one(n, carry):
                side = n // each
                at = n % each
                row = pl.multiple_of((at // across) * row_tile, BLOCK)
                column = pl.multiple_of((at % across) * column_tile, BLOCK)
                slot = (done + n) % slots
                to_row, to_column = place(side, row, column)
                target = out_ref.at[pl.ds(to_row, row_tile), pl.ds(to_column, column_tile)]

                def free():
                    copy(slot, target).wait()

                if done >= slots:
                    free()
                else:
                    pl.when(done + n >= slots)(free)
                lhs = left(side, row)
                for c in range(0, column_tile, chunk):
                    size = min(chunk, column_tile - c)
                    tile = contract(lhs, right(side, column, c, size), 1, 0).astype(B16)
                    tile = keep_blocks(
                        tile,
                        lambda i, j: mask_ref(to_row // BLOCK + i, (to_column + c) // BLOCK + j),
                    )
                    ring[slot, :, c : c + size] = tile
                copy(slot, target).start()
                return carry

            lax.fori_loop(0, 2 * each, one, 0)
            return done + 2 * each

        done = tiles(
            0, down_out, lambda i, j: down_mask_ref[i, j], depth, width, tall, wide,
            lambda side, row: grads_turned[pl.ds(row, tall), :],
            lambda side, column, c, size: hidden_all[side, :, pl.ds(pl.multiple_of(column + c, BLOCK), size)],
            lambda side, row, column: (row, pl.multiple_of(half_of_pair(side) * width + column, BLOCK)),
        )
        for kind, out_ref, mask in ((0, gate_out, gate_mask_ref), (1, up_out, up_mask_ref)):
            done = tiles(
                done, out_ref, lambda i, j: mask[j, i], width, depth, tall, wide,
                lambda side, row: turned[kind, side, pl.ds(row, tall), :],
                lambda side, column, c, size: tokens_all[:, pl.ds(pl.multiple_of(column + c, BLOCK), size)],
                lambda side, row, column: (pl.multiple_of(half_of_pair(side) * width + row, BLOCK), column),
            )
        for slot in range(min(slots, done)):
            copy(slot, up_out.at[pl.ds(0, tall), pl.ds(0, wide)]).wait()

    return pl.pallas_call(
        kernel,
        name="weight_grads",
        in_specs=[SMEM] * 3 + [VMEM] * (4 + parts),
        out_specs=[ANY] * 3,
        out_shape=[
            jax.ShapeDtypeStruct((2 * width, depth), B16),
            jax.ShapeDtypeStruct((2 * width, depth), B16),
            jax.ShapeDtypeStruct((depth, 2 * width), B16),
        ],
        scratch_shapes=[
            pltpu.VMEM((slots, tall, wide), B16),
            pltpu.SemaphoreType.DMA((slots,)),
            pltpu.VMEM((2, count, width), B16),
            pltpu.VMEM((2, 2, width, count), B16),
            pltpu.VMEM((count, depth), B16),
            pltpu.VMEM((depth, count), B16),
        ],
        compiler_params=params(24),
        cost_estimate=cost(0, 12 * width * depth),
    )(masks[0].T, masks[1].T, masks[2], *hidden, *delta, *joint)


def body(rows, tokens, output_grad, gate_weight, up_weight, down_weight, gate_mask, up_mask, down_mask):
    masks = (gate_mask, up_mask, down_mask)
    direct = rows <= 4
    pieces = 2 if gate_weight.shape[0] >= 2048 else 1

    def gather(array):
        if not direct:
            return list(lax.all_gather(array, "row", axis=0))
        return [array] + [
            lax.ppermute(array, "row", [(i, (i + s) % rows) for i in range(rows)])
            for s in range(1, rows)
        ]

    def swap(array, bit):
        size = lax.axis_size("col")
        return lax.ppermute(array, "col", [(i, i ^ bit) for i in range(size)])

    joint = gather(join(tokens, output_grad))
    gate_w, up_w, down_w = load(((gate_weight, 0), (up_weight, 0), (down_weight, 1)), pieces)

    gate_sent = up_forward(FAR, gate_mask, gate_w[FAR], joint)
    up_sent = up_forward(FAR, up_mask, up_w[FAR], joint)
    delta_sent = down_forward(FAR, down_mask, down_w[FAR], joint)
    gate = up_forward(OWN, gate_mask, gate_w[OWN], joint, swap(gate_sent, 1))
    gate_far = swap(gate, 2)
    up = up_forward(OWN, up_mask, up_w[OWN], joint, swap(up_sent, 1))
    up_far = swap(up, 2)
    delta = down_forward(OWN, down_mask, down_w[OWN], joint, swap(delta_sent, 1))
    delta_far = swap(delta, 2)

    hidden = activate(gate, gate_far, up, up_far)
    hidden = (hidden, swap(hidden, 1))
    out = output_part(OWN, down_mask, down_w[OWN], hidden[OWN], after=[delta])
    both = deltas(gate, gate_far, up, up_far, delta, delta_far, after=[out])
    out = output_part(FAR, down_mask, down_w[FAR], hidden[FAR], out, after=[both])
    both = (both, swap(both, 1))
    first = input_part(OWN, masks, gate_w[OWN], up_w[OWN], both[OWN])
    blocks = input_part(
        FAR, masks, gate_w[FAR], up_w[FAR], both[FAR], first[0], out, rows if direct else 1
    )
    count = tokens.shape[0]
    if direct:
        parts = [blocks[0]]
        for s in range(1, rows):
            parts.append(lax.ppermute(blocks[s], "row", [(i, (i - s) % rows) for i in range(rows)]))
        summed = total(p.astype(F32) for p in parts).astype(B16)
        output, input_grad = summed[:count], summed[count:]
    else:
        half = blocks[0].shape[0] // 2
        output, input_grad = [
            lax.psum_scatter(part, "row", scatter_dimension=0, tiled=True)
            for part in (blocks[0][:half], blocks[0][half:])
        ]
    gate_grad, up_grad, down_grad = weight_grads(masks, joint, hidden, both)
    return output, input_grad, gate_grad, up_grad, down_grad


def solution(mesh):
    rows = mesh.shape["row"]
    held = P(("member", "row"), "col")
    down_held = P(("member", "col"), "row")
    return jax.shard_map(
        functools.partial(body, rows),
        mesh=mesh,
        in_specs=(held, held, held, held, down_held, P("row", "col"), P("row", "col"), P("col", "row")),
        out_specs=(held, held, held, held, down_held),
        check_vma=False,
    )
```

profile of v0, /device:TPU:0, one launch (start us, length us, event | category | flops | bytes accessed | tf_op | source)
XLA Modules:
  0.0 91.9 jit_solution(17365953457073926049)
XLA Ops:
  0.6 0.9 join.1.rest_2_.rest_4_
  1.5 5.1 %collective-permute-start.2 = (bf16[32,2048]{1,0:T(8,128)(2,1)S(1)}, bf16[32,2048]{1,0:T(8,128)(2,1)S(1)}, u32[]{:S(2)}, u32[]{:S(2)}) collective-permute-start(bf16[32,2048]{1,0:T(8,128)(2,1)S(1)} %join.1.rest_2_.rest_4_), channel_id=1, source_target_pairs={{0,12},{4,0},{8,4},{12,8},{1,13},{5,1},{9,5},{13,9},{2,14},{6,2},{... | collective-permute-start | bytes 393224 | tf_op jit(solution)/shard_map/ppermute | solution.py:526
  6.6 1.0 %collective-permute-start = (bf16[32,2048]{1,0:T(8,128)(2,1)S(1)}, bf16[32,2048]{1,0:T(8,128)(2,1)S(1)}, u32[]{:S(2)}, u32[]{:S(2)}) collective-permute-start(bf16[32,2048]{1,0:T(8,128)(2,1)S(1)} %join.1.rest_2_.rest_4_), channel_id=1, source_target_pairs={{0,4},{4,8},{8,12},{12,0},{1,5},{5,9},{9,13},{13,1},{2,6},{6,10},{... | collective-permute-start | bytes 393224 | tf_op jit(solution)/shard_map/ppermute | solution.py:526
  7.7 15.6 %load.1 = (bf16[1024,2048]{1,0:T(8,128)(2,1)S(1)}, bf16[1024,2048]{1,0:T(8,128)(2,1)S(1)}, bf16[1024,2048]{1,0:T(8,128)(2,1)S(1)}, bf16[1024,2048]{1,0:T(8,128)(...) custom-call(bf16[4096,2048]{1,0:T(8,128)(2,1)} %refs_0_.1, ...), custom_call_target="tpu_custom_call" | custom-call | bytes 50331648 | tf_op jit(solution)/shard_map/load/pallas_call | solution.py:138
  23.2 0.0 copy-start.2
  23.3 3.1 %up_forward.6 = bf16[64,2048]{1,0:T(8,128)(2,1)S(1)} custom-call(s32[16,32]{1,0:T(8,128)S(1)} %bitcast.7, bf16[1024,2048]{1,0:T(8,128)(2,1)S(1)} %get-tuple-element.26.rest_0_.rest_2_, bf16[1024,2048]{1,0:T(8,128)(2,1)S(1)} %get-tuple-element.27.rest_1_.rest_3_, bf16[32,2048]{1,0:T(8,128)(2,1)S(1)} %join.1.rest_2_.rest_4_, ...), custom_call_target="tpu_custom_call" | custom-call | flops 1 | bytes 1 | tf_op jit(solution)/shard_map/up_forward/pallas_call | solution.py:247
  26.4 0.1 collective-permute-start.5
  26.5 3.1 %up_forward.4 = bf16[64,2048]{1,0:T(8,128)(2,1)S(1)} custom-call(s32[16,32]{1,0:T(8,128)S(1)} %bitcast.2, bf16[1024,2048]{1,0:T(8,128)(2,1)S(1)} %get-tuple-element.24.rest_0_, bf16[1024,2048]{1,0:T(8,128)(2,1)S(1)} %get-tuple-element.25.rest_1_, bf16[32,2048]{1,0:T(8,128)(2,1)S(1)} %join.1.rest_2_.rest_4_, ...), custom_call_target="tpu_custom_call" | custom-call | flops 1 | bytes 1 | tf_op jit(solution)/shard_map/up_forward/pallas_call | solution.py:247
  29.7 0.5 collective-permute-start.3
  30.2 2.2 %down_forward.2 = bf16[64,2048]{1,0:T(8,128)(2,1)S(1)} custom-call(s32[16,32]{1,0:T(8,128)S(1)} %copy-done.6, bf16[2048,1024]{1,0:T(8,128)(2,1)S(1)} %get-tuple-element.34.rest_0_, bf16[2048,1024]{1,0:T(8,128)(2,1)S(1)} %get-tuple-element.35.rest_1_, bf16[32,2048]{1,0:T(8,128)(2,1)S(1)} %join.1.rest_2_.rest_4_, ...), custom_call_target="tpu_custom_call" | custom-call | flops 1 | bytes 1 | tf_op jit(solution)/shard_map/down_forward/pallas_call | solution.py:191
  32.5 0.1 collective-permute-start.7
  32.6 3.2 %up_forward.7.up_ref = bf16[64,2048]{1,0:T(8,128)(2,1)S(1)} custom-call(s32[16,32]{1,0:T(8,128)S(1)} %bitcast.8, bf16[1024,2048]{1,0:T(8,128)(2,1)S(1)} %get-tuple-element.30.rest_0_.rest_2_, bf16[1024,2048]{1,0:T(8,128)(2,1)S(1)} %get-tuple-element.31.rest_1_.rest_3_, bf16[32,2048]{1,0:T(8,128)(2,1)S(1)} %join.1.rest_2_.rest_4_, ...), custom_call_target="tpu_custom_call" | custom-call | flops 1 | bytes 1 | tf_op jit(solution)/shard_map/up_forward/pallas_call | solution.py:247
  35.8 1.6 %collective-permute-start.6 = (bf16[64,2048]{1,0:T(8,128)(2,1)S(1)}, bf16[64,2048]{1,0:T(8,128)(2,1)S(1)}, u32[]{:S(2)}, u32[]{:S(2)}) collective-permute-start(bf16[64,2048]{1,0:T(8,128)(2,1)S(1)} %up_forward.7.up_ref), channel_id=1, source_target_pairs={{0,2},{1,3},{2,0},{3,1},{4,6},{5,7},{6,4},{7,5},{8,10},{9,11},{10,... | collective-permute-start | bytes 786440 | tf_op jit(solution)/shard_map/ppermute | solution.py:532
  37.3 3.2 %up_forward.5.gate_ref = bf16[64,2048]{1,0:T(8,128)(2,1)S(1)} custom-call(s32[16,32]{1,0:T(8,128)S(1)} %bitcast.3, bf16[1024,2048]{1,0:T(8,128)(2,1)S(1)} %get-tuple-element.28.rest_0_, bf16[1024,2048]{1,0:T(8,128)(2,1)S(1)} %get-tuple-element.29.rest_1_, bf16[32,2048]{1,0:T(8,128)(2,1)S(1)} %join.1.rest_2_.rest_4_, ...), custom_call_target="tpu_custom_call" | custom-call | flops 1 | bytes 1 | tf_op jit(solution)/shard_map/up_forward/pallas_call | solution.py:247
  40.5 0.6 collective-permute-start.4
  41.1 2.4 %down_forward.3.rest_3_.delta_ref = bf16[64,2048]{1,0:T(8,128)(2,1)S(1)} custom-call(s32[16,32]{1,0:T(8,128)S(1)} %copy-done.6, bf16[2048,1024]{1,0:T(8,128)(2,1)S(1)} %get-tuple-element.32.rest_0_, bf16[2048,1024]{1,0:T(8,128)(2,1)S(1)} %get-tuple-element.33.rest_1_, bf16[32,2048]{1,0:T(8,128)(2,1)S(1)} %join.1.rest_2_.rest_4_, ...), custom_call_target="tpu_custom_call" | custom-call | flops 1 | bytes 1 | tf_op jit(solution)/shard_map/down_forward/pallas_call | solution.py:191
  43.5 1.6 %collective-permute-start.8 = (bf16[64,2048]{1,0:T(8,128)(2,1)S(1)}, bf16[64,2048]{1,0:T(8,128)(2,1)S(1)}, u32[]{:S(2)}, u32[]{:S(2)}) collective-permute-start(bf16[64,2048]{1,0:T(8,128)(2,1)S(1)} %down_forward.3.rest_3_.delta_ref), channel_id=1, source_target_pairs={{0,2},{1,3},{2,0},{3,1},{4,6},{5,7},{6,4},{7,5},{8,10},{9,11},{10,... | collective-permute-start | bytes 786440 | tf_op jit(solution)/shard_map/ppermute | solution.py:532
  45.1 5.4 %collective-permute-done.4.gate_far_ref = bf16[64,2048]{1,0:T(8,128)(2,1)S(1)} collective-permute-done((bf16[64,2048]{1,0:T(8,128)(2,1)S(1)}, bf16[64,2048]{1,0:T(8,128)(2,1)S(1)}, u32[]{:S(2)}, u32[]{:S(2)}) %collective-permute-start.4) | collective-permute-done | bytes 262176 | tf_op jit(solution)/shard_map/ppermute | solution.py:532
  50.6 0.2 activate.1.rest_2_.rest_0_
  50.8 3.6 %output_part.2.rest_0_.rest_3_ = f32[64,2048]{1,0:T(8,128)S(1)} custom-call(s32[16,32]{1,0:T(8,128)S(1)} %copy-done.6, bf16[2048,1024]{1,0:T(8,128)(2,1)S(1)} %get-tuple-element.32.rest_0_, bf16[2048,1024]{1,0:T(8,128)(2,1)S(1)} %get-tuple-element.33.rest_1_, bf16[64,2048]{1,0:T(8,128)(2,1)S(1)} %activate.1.rest_2_.rest_0_, ...), custom_call_target="tpu_custom_call" | custom-call | flops 1 | bytes 1 | tf_op jit(solution)/shard_map/output_part/pallas_call | solution.py:344
  54.3 1.4 %collective-permute-done.8.delta_far_ref = bf16[64,2048]{1,0:T(8,128)(2,1)S(1)} collective-permute-done((bf16[64,2048]{1,0:T(8,128)(2,1)S(1)}, bf16[64,2048]{1,0:T(8,128)(2,1)S(1)}, u32[]{:S(2)}, u32[]{:S(2)}) %collective-permute-start.8) | collective-permute-done | bytes 262176 | tf_op jit(solution)/shard_map/ppermute | solution.py:532
  55.7 0.4 deltas.1.rest_4_.rest_2_
  56.1 0.1 collective-permute-start.9
  56.2 0.5 collective-permute-start.10
  56.7 3.9 %input_part.2.rest_5_ = f32[64,2048]{1,0:T(8,128)S(1)} custom-call(s32[16,32]{1,0:T(8,128)S(1)} %bitcast.4, s32[16,32]{1,0:T(8,128)S(1)} %bitcast.9, bf16[1024,2048]{1,0:T(8,128)(2,1)S(1)} %get-tuple-element.28.rest_0_, bf16[1024,2048]{1,0:T(8,128)(2,1)S(1)} %get-tuple-element.29.rest_1_, bf16[1024,2048]{1,0:T(8,128)(2,1)S(1)} %get-tuple-element.30.rest_0_.rest_2_, ...), custom_call_target="tpu_custom_call" | custom-call | flops 4294967296 | tf_op jit(solution)/shard_map/input_part/pallas_call | solution.py:407
  60.6 3.6 %output_part.3.rest_6_ = f32[64,2048]{1,0:T(8,128)S(1)} custom-call(s32[16,32]{1,0:T(8,128)S(1)} %copy-done.6, bf16[2048,1024]{1,0:T(8,128)(2,1)S(1)} %get-tuple-element.34.rest_0_, bf16[2048,1024]{1,0:T(8,128)(2,1)S(1)} %get-tuple-element.35.rest_1_, bf16[64,2048]{1,0:T(8,128)(2,1)S(1)} %collective-permute-done.10.rest_2_.rest_1_, ...), custom_call_target="tpu_custom_call" | custom-call | flops 1 | bytes 1 | tf_op jit(solution)/shard_map/output_part/pallas_call | solution.py:344
  64.2 3.9 %input_part.3 = (bf16[32,2048]{1,0:T(8,128)(2,1)S(1)}, bf16[32,2048]{1,0:T(8,128)(2,1)S(1)}, bf16[32,2048]{1,0:T(8,128)(2,1)S(1)}, bf16[32,2048]{1,0:T(8,128)(2,1)S(1)}) custom-call(s32[16,32]{1,0:T(8,128)S(1)} %bitcast.5, s32[16,32]{1,0:T(8,128)S(1)} %bitcast.10, bf16[1024,2048]{1,0:T(8,128)(2,1)S(1)} %get-tuple-element.24.rest_0_, ...), custom_call_target="tpu_custom_call" | custom-call | flops 4294967296 | tf_op jit(solution)/shard_map/input_part/pallas_call | solution.py:407
  68.2 2.9 %collective-permute-start.11 = (bf16[32,2048]{1,0:T(8,128)(2,1)S(1)}, bf16[32,2048]{1,0:T(8,128)(2,1)S(1)}, u32[]{:S(2)}, u32[]{:S(2)}) collective-permute-start(bf16[32,2048]{1,0:T(8,128)(2,1)S(1)} %get-tuple-element.37), channel_id=1, source_target_pairs={{0,12},{4,0},{8,4},{12,8},{1,13},{5,1},{9,5},{13,9},{2,14},{6,2},{... | collective-permute-start | bytes 393224 | tf_op jit(solution)/shard_map/ppermute | solution.py:561
  71.0 1.1 %collective-permute-start.12 = (bf16[32,2048]{1,0:T(8,128)(2,1)S(1)}, bf16[32,2048]{1,0:T(8,128)(2,1)S(1)}, u32[]{:S(2)}, u32[]{:S(2)}) collective-permute-start(bf16[32,2048]{1,0:T(8,128)(2,1)S(1)} %get-tuple-element.38), channel_id=1, source_target_pairs={{0,8},{4,12},{8,0},{12,4},{1,9},{5,13},{9,1},{13,5},{2,10},{6,14},... | collective-permute-start | bytes 393224 | tf_op jit(solution)/shard_map/ppermute | solution.py:561
  72.1 19.0 %weight_grads.1 = (bf16[4096,2048]{1,0:T(8,128)(2,1)}, bf16[4096,2048]{1,0:T(8,128)(2,1)}, bf16[2048,4096]{1,0:T(8,128)(2,1)}) custom-call(s32[16,32]{1,0:T(8,128)S(1)} %bitcast.6, s32[16,32]{1,0:T(8,128)S(1)} %bitcast.11, s32[16,32]{1,0:T(8,128)S(1)} %copy-done.6, bf16[64,2048]{1,0:T(8,128)(2,1)S(1)} %activate.1.rest_2_.rest_0_, ...), custom_call_target="tpu_custom_call" | custom-call | bytes 50331648 | tf_op jit(solution)/shard_map/weight_grads/pallas_call | solution.py:494
  91.2 0.1 add_convert_fusion
  91.2 0.7 fusion
  (27 shorter events, 0.1 us)
Async XLA Ops:
  1.5 21.7 %copy-start.5 = (s32[32,16]{0,1:T(8,128)S(1)}, s32[32,16]{0,1:T(8,128)}, u32[]{:S(2)}) copy-start(s32[32,16]{0,1:T(8,128)} %param.14) | copy-start | bytes 6148
  1.5 21.7 %collective-permute-start.2 = (bf16[32,2048]{1,0:T(8,128)(2,1)S(1)}, bf16[32,2048]{1,0:T(8,128)(2,1)S(1)}, u32[]{:S(2)}, u32[]{:S(2)}) collective-permute-start(bf16[32,2048]{1,0:T(8,128)(2,1)S(1)} %join.1.rest_2_.rest_4_), channel_id=1, source_target_pairs={{0,12},{4,0},{8,4},{12,8},{1,13},{5,1},{9,5},{13,9},{2,14},{6,2},{... | collective-permute-start | bytes 393224 | tf_op jit(solution)/shard_map/ppermute | solution.py:526
  6.6 16.6 %collective-permute-start.1 = (bf16[32,2048]{1,0:T(8,128)(2,1)S(1)}, bf16[32,2048]{1,0:T(8,128)(2,1)S(1)}, u32[]{:S(2)}, u32[]{:S(2)}) collective-permute-start(bf16[32,2048]{1,0:T(8,128)(2,1)S(1)} %join.1.rest_2_.rest_4_), channel_id=1, source_target_pairs={{0,8},{4,12},{8,0},{12,4},{1,9},{5,13},{9,1},{13,5},{2,10},{6,14},... | collective-permute-start | bytes 393224 | tf_op jit(solution)/shard_map/ppermute | solution.py:526
  6.6 16.6 %collective-permute-start = (bf16[32,2048]{1,0:T(8,128)(2,1)S(1)}, bf16[32,2048]{1,0:T(8,128)(2,1)S(1)}, u32[]{:S(2)}, u32[]{:S(2)}) collective-permute-start(bf16[32,2048]{1,0:T(8,128)(2,1)S(1)} %join.1.rest_2_.rest_4_), channel_id=1, source_target_pairs={{0,4},{4,8},{8,12},{12,0},{1,5},{5,9},{9,13},{13,1},{2,6},{6,10},{... | collective-permute-start | bytes 393224 | tf_op jit(solution)/shard_map/ppermute | solution.py:526
  23.2 3.3 %copy-start.2 = (bf16[1024,2048]{1,0:T(8,128)(2,1)}, bf16[1024,2048]{1,0:T(8,128)(2,1)S(1)}, u32[]{:S(2)}) copy-start(bf16[1024,2048]{1,0:T(8,128)(2,1)S(1)} %get-tuple-element.25.rest_1_) | copy-start | bytes 12582916
  23.2 9.3 %copy-start = (bf16[1024,2048]{1,0:T(8,128)(2,1)}, bf16[1024,2048]{1,0:T(8,128)(2,1)S(1)}, u32[]{:S(2)}) copy-start(bf16[1024,2048]{1,0:T(8,128)(2,1)S(1)} %get-tuple-element.31.rest_1_.rest_3_) | copy-start | bytes 12582916
  23.3 3.2 %copy-start.4 = (s32[32,16]{0,1:T(8,128)S(1)}, s32[32,16]{0,1:T(8,128)}, u32[]{:S(2)}) copy-start(s32[32,16]{0,1:T(8,128)} %param.13) | copy-start | bytes 6148
  26.4 6.1 %collective-permute-start.5 = (bf16[64,2048]{1,0:T(8,128)(2,1)S(1)}, bf16[64,2048]{1,0:T(8,128)(2,1)S(1)}, u32[]{:S(2)}, u32[]{:S(2)}) collective-permute-start(bf16[64,2048]{1,0:T(8,128)(2,1)S(1)} %up_forward.6), channel_id=1, source_target_pairs={{0,1},{1,0},{2,3},{3,2},{4,5},{5,4},{6,7},{7,6},{8,9},{9,8},{10,11... | collective-permute-start | bytes 786440 | tf_op jit(solution)/shard_map/ppermute | solution.py:532
  26.5 3.7 %copy-start.6 = (s32[16,32]{1,0:T(8,128)S(1)}, s32[16,32]{1,0:T(8,128)}, u32[]{:S(2)}) copy-start(s32[16,32]{1,0:T(8,128)} %down_mask_ref.1) | copy-start | bytes 6148
  29.7 7.6 %collective-permute-start.3 = (bf16[64,2048]{1,0:T(8,128)(2,1)S(1)}, bf16[64,2048]{1,0:T(8,128)(2,1)S(1)}, u32[]{:S(2)}, u32[]{:S(2)}) collective-permute-start(bf16[64,2048]{1,0:T(8,128)(2,1)S(1)} %up_forward.4), channel_id=1, source_target_pairs={{0,1},{1,0},{2,3},{3,2},{4,5},{5,4},{6,7},{7,6},{8,9},{9,8},{10,11... | collective-permute-start | bytes 786440 | tf_op jit(solution)/shard_map/ppermute | solution.py:532
  32.5 8.7 %collective-permute-start.7 = (bf16[64,2048]{1,0:T(8,128)(2,1)S(1)}, bf16[64,2048]{1,0:T(8,128)(2,1)S(1)}, u32[]{:S(2)}, u32[]{:S(2)}) collective-permute-start(bf16[64,2048]{1,0:T(8,128)(2,1)S(1)} %down_forward.2), channel_id=1, source_target_pairs={{0,1},{1,0},{2,3},{3,2},{4,5},{5,4},{6,7},{7,6},{8,9},{9,8},{10,11... | collective-permute-start | bytes 786440 | tf_op jit(solution)/shard_map/ppermute | solution.py:532
  35.8 9.3 %collective-permute-start.6 = (bf16[64,2048]{1,0:T(8,128)(2,1)S(1)}, bf16[64,2048]{1,0:T(8,128)(2,1)S(1)}, u32[]{:S(2)}, u32[]{:S(2)}) collective-permute-start(bf16[64,2048]{1,0:T(8,128)(2,1)S(1)} %up_forward.7.up_ref), channel_id=1, source_target_pairs={{0,2},{1,3},{2,0},{3,1},{4,6},{5,7},{6,4},{7,5},{8,10},{9,11},{10,... | collective-permute-start | bytes 786440 | tf_op jit(solution)/shard_map/ppermute | solution.py:532
  40.5 10.0 %collective-permute-start.4 = (bf16[64,2048]{1,0:T(8,128)(2,1)S(1)}, bf16[64,2048]{1,0:T(8,128)(2,1)S(1)}, u32[]{:S(2)}, u32[]{:S(2)}) collective-permute-start(bf16[64,2048]{1,0:T(8,128)(2,1)S(1)} %up_forward.5.gate_ref), channel_id=1, source_target_pairs={{0,2},{1,3},{2,0},{3,1},{4,6},{5,7},{6,4},{7,5},{8,10},{9,11},{10,... | collective-permute-start | bytes 786440 | tf_op jit(solution)/shard_map/ppermute | solution.py:532
  43.5 12.2 %collective-permute-start.8 = (bf16[64,2048]{1,0:T(8,128)(2,1)S(1)}, bf16[64,2048]{1,0:T(8,128)(2,1)S(1)}, u32[]{:S(2)}, u32[]{:S(2)}) collective-permute-start(bf16[64,2048]{1,0:T(8,128)(2,1)S(1)} %down_forward.3.rest_3_.delta_ref), channel_id=1, source_target_pairs={{0,2},{1,3},{2,0},{3,1},{4,6},{5,7},{6,4},{7,5},{8,10},{9,11},{10,... | collective-permute-start | bytes 786440 | tf_op jit(solution)/shard_map/ppermute | solution.py:532
  50.7 5.9 %copy-start.1 = (bf16[1024,2048]{1,0:T(8,128)(2,1)S(1)}, bf16[1024,2048]{1,0:T(8,128)(2,1)}, u32[]{:S(2)}) copy-start(bf16[1024,2048]{1,0:T(8,128)(2,1)} %copy-done) | copy-start | bytes 12582916
  56.1 8.1 %collective-permute-start.9 = (bf16[128,2048]{1,0:T(8,128)(2,1)S(1)}, bf16[128,2048]{1,0:T(8,128)(2,1)S(1)}, u32[]{:S(2)}, u32[]{:S(2)}) collective-permute-start(bf16[128,2048]{1,0:T(8,128)(2,1)S(1)} %deltas.1.rest_4_.rest_2_), channel_id=1, source_target_pairs={{0,1},{1,0},{2,3},{3,2},{4,5},{5,4},{6,7},{7,6},{8,9},{9,8},{10,11... | collective-permute-start | bytes 1572872 | tf_op jit(solution)/shard_map/ppermute | solution.py:532
  56.2 4.4 %collective-permute-start.10 = (bf16[64,2048]{1,0:T(8,128)(2,1)S(1)}, bf16[64,2048]{1,0:T(8,128)(2,1)S(1)}, u32[]{:S(2)}, u32[]{:S(2)}) collective-permute-start(bf16[64,2048]{1,0:T(8,128)(2,1)S(1)} %activate.1.rest_2_.rest_0_), channel_id=1, source_target_pairs={{0,1},{1,0},{2,3},{3,2},{4,5},{5,4},{6,7},{7,6},{8,9},{9,8},{10,11... | collective-permute-start | bytes 786440 | tf_op jit(solution)/shard_map/ppermute | solution.py:532
  60.6 3.6 %copy-start.3 = (bf16[1024,2048]{1,0:T(8,128)(2,1)S(1)}, bf16[1024,2048]{1,0:T(8,128)(2,1)}, u32[]{:S(2)}) copy-start(bf16[1024,2048]{1,0:T(8,128)(2,1)} %copy-done.2) | copy-start | bytes 12582916
  68.2 23.0 %collective-permute-start.11 = (bf16[32,2048]{1,0:T(8,128)(2,1)S(1)}, bf16[32,2048]{1,0:T(8,128)(2,1)S(1)}, u32[]{:S(2)}, u32[]{:S(2)}) collective-permute-start(bf16[32,2048]{1,0:T(8,128)(2,1)S(1)} %get-tuple-element.37), channel_id=1, source_target_pairs={{0,12},{4,0},{8,4},{12,8},{1,13},{5,1},{9,5},{13,9},{2,14},{6,2},{... | collective-permute-start | bytes 393224 | tf_op jit(solution)/shard_map/ppermute | solution.py:561
  71.0 20.1 %collective-permute-start.12 = (bf16[32,2048]{1,0:T(8,128)(2,1)S(1)}, bf16[32,2048]{1,0:T(8,128)(2,1)S(1)}, u32[]{:S(2)}, u32[]{:S(2)}) collective-permute-start(bf16[32,2048]{1,0:T(8,128)(2,1)S(1)} %get-tuple-element.38), channel_id=1, source_target_pairs={{0,8},{4,12},{8,0},{12,4},{1,9},{5,13},{9,1},{13,5},{2,10},{6,14},... | collective-permute-start | bytes 393224 | tf_op jit(solution)/shard_map/ppermute | solution.py:561
  72.1 19.0 %collective-permute-start.13 = (bf16[32,2048]{1,0:T(8,128)(2,1)S(1)}, bf16[32,2048]{1,0:T(8,128)(2,1)S(1)}, u32[]{:S(2)}, u32[]{:S(2)}) collective-permute-start(bf16[32,2048]{1,0:T(8,128)(2,1)S(1)} %get-tuple-element.39), channel_id=1, source_target_pairs={{0,4},{4,8},{8,12},{12,0},{1,5},{5,9},{9,13},{13,1},{2,6},{6,10},{... | collective-permute-start | bytes 393224 | tf_op jit(solution)/shard_map/ppermute | solution.py:561
where the time goes:
time: 92.1 us; the launch traced here: 91.9 us
  Pallas kernels  68.2 us (74%)
  starting transfers between devices  15.1 us (16%)
  waiting for transfers between devices  6.9 us (7%)
    pallas_call x1, Pallas kernels, weight_grads(): pl.pallas_call(kernel, name='weight_grads', in_specs=[SMEM] * 3 + [VMEM]...  19 us
    pallas_call x1, Pallas kernels, load(): pl.pallas_call(kernel, name='load', in_specs=[ANY] * count, out_specs=[VM...  15.6 us
    pallas_call x4, Pallas kernels, up_forward(): pl.pallas_call(kernel, name='up_forward', in_specs=[SMEM] + [VMEM] * (pie...  12.6 us
    pallas_call x2, Pallas kernels, input_part(): pl.pallas_call(kernel, name='input_part', in_specs=[SMEM] * 2 + [VMEM] *...  7.82 us
    pallas_call x2, Pallas kernels, output_part(): pl.pallas_call(kernel, name='output_part', in_specs=[SMEM] + [VMEM] * (pi...  7.15 us
    ppermute x8, waiting for transfers between devices, swap(): return lax.ppermute(array, 'col', [(i, i ^ bit) for i in range(size)])  6.89 us
    ppermute x3, starting transfers between devices, gather(): lax.ppermute(array, 'row', [(i, (i + s) % rows) for i in range(rows)])  6.11 us
    ppermute x8, starting transfers between devices, swap(): return lax.ppermute(array, 'col', [(i, i ^ bit) for i in range(size)])  5 us
  transfers between devices with their start and end apart: 14, of which 2 were waited for; matrix products, arithmetic and copies ran while one was open for 0% of the time, Pallas kernels for 65%

commit v1 on v0

--- a/solution.py
+++ b/solution.py
@@ -116,12 +116,12 @@
     return pltpu.with_memory_space_constraint(array, pltpu.HBM)
 
 
-def load(items, pieces):
+def load(items, pieces, after=()):
     count = len(items)
     shapes = [s for weight, dim in items for s in piece_shapes(weight, dim, pieces) * 2]
 
     def kernel(*refs):
-        outs, sems = refs[count:-1], refs[-1]
+        outs, sems = refs[count + len(after) : -1], refs[-1]
         copies = []
         for n, (_, dim) in enumerate(items):
             for side in (OWN, FAR):
@@ -138,13 +138,13 @@
     loaded = pl.pallas_call(
         kernel,
         name="load",
-        in_specs=[ANY] * count,
+        in_specs=[ANY] * (count + len(after)),
         out_specs=[VMEM] * len(shapes),
         out_shape=[pltpu.VMEM(s, B16) for s in shapes],
         scratch_shapes=[pltpu.SemaphoreType.DMA((len(shapes) * CUTS,))],
         compiler_params=params(1),
-        cost_estimate=cost(0, sum(w.size * 2 for w, _ in items)),
-    )(*[in_hbm(w) for w, _ in items])
+        cost_estimate=cost(1, 1) if after else cost(0, sum(w.size * 2 for w, _ in items)),
+    )(*[in_hbm(w) for w, _ in items], *after)
     return [
         [loaded[(2 * n + side) * pieces : (2 * n + side + 1) * pieces] for side in (OWN, FAR)]
         for n in range(count)
@@ -255,8 +255,9 @@
     )(mask.T, *resident(weight), *tokens, *more, *after)
 
 
-def activate(gate, gate_far, up, up_far):
-    def kernel(gate_ref, gate_far_ref, up_ref, up_far_ref, out_ref):
+def activate(gate, gate_far, up, up_far, after=()):
+    def kernel(gate_ref, gate_far_ref, up_ref, up_far_ref, *rest):
+        out_ref = rest[-1]
         gate_sum = gate_ref[...].astype(F32) + gate_far_ref[...].astype(F32)
         up_sum = up_ref[...].astype(F32) + up_far_ref[...].astype(F32)
         out_ref[...] = (gate_sum * jax.nn.sigmoid(gate_sum) * up_sum).astype(B16)
@@ -264,12 +265,12 @@
     return pl.pallas_call(
         kernel,
         name="activate",
-        in_specs=[VMEM] * 4,
+        in_specs=[VMEM] * 4 + [ANY] * len(after),
         out_specs=VMEM,
         out_shape=jax.ShapeDtypeStruct(gate.shape, B16),
         compiler_params=params(4),
         cost_estimate=cost(gate.size * 300, 0),
-    )(gate, gate_far, up, up_far)
+    )(gate, gate_far, up, up_far, *after)
 
 
 def deltas(gate, gate_far, up, up_far, delta, delta_far, after=()):
@@ -532,23 +533,24 @@
         return lax.ppermute(array, "col", [(i, i ^ bit) for i in range(size)])
 
     joint = gather(join(tokens, output_grad))
-    gate_w, up_w, down_w = load(((gate_weight, 0), (up_weight, 0), (down_weight, 1)), pieces)
+    gate_w, up_w = load(((gate_weight, 0), (up_weight, 0)), pieces)
 
     gate_sent = up_forward(FAR, gate_mask, gate_w[FAR], joint)
-    up_sent = up_forward(FAR, up_mask, up_w[FAR], joint)
-    delta_sent = down_forward(FAR, down_mask, down_w[FAR], joint)
-    gate = up_forward(OWN, gate_mask, gate_w[OWN], joint, swap(gate_sent, 1))
+    up_sent = up_forward(FAR, up_mask, up_w[FAR], joint, after=[gate_sent])
+    gate = up_forward(OWN, gate_mask, gate_w[OWN], joint, swap(gate_sent, 1), after=[up_sent])
     gate_far = swap(gate, 2)
-    up = up_forward(OWN, up_mask, up_w[OWN], joint, swap(up_sent, 1))
+    up = up_forward(OWN, up_mask, up_w[OWN], joint, swap(up_sent, 1), after=[gate])
     up_far = swap(up, 2)
-    delta = down_forward(OWN, down_mask, down_w[OWN], joint, swap(delta_sent, 1))
+    (down_w,) = load(((down_weight, 1),), pieces, after=[up])
+    delta_sent = down_forward(FAR, down_mask, down_w[FAR], joint, after=[gate_far])
+    hidden = activate(gate, gate_far, up, up_far, after=[delta_sent])
+    hidden = (hidden, swap(hidden, 1))
+    delta = down_forward(OWN, down_mask, down_w[OWN], joint, swap(delta_sent, 1), after=[hidden[OWN]])
     delta_far = swap(delta, 2)
 
-    hidden = activate(gate, gate_far, up, up_far)
-    hidden = (hidden, swap(hidden, 1))
     out = output_part(OWN, down_mask, down_w[OWN], hidden[OWN], after=[delta])
+    out = output_part(FAR, down_mask, down_w[FAR], hidden[FAR], out)
     both = deltas(gate, gate_far, up, up_far, delta, delta_far, after=[out])
-    out = output_part(FAR, down_mask, down_w[FAR], hidden[FAR], out, after=[both])
     both = (both, swap(both, 1))
     first = input_part(OWN, masks, gate_w[OWN], up_w[OWN], both[OWN])
     blocks = input_part(

time: 92.1 us -> 87.3 us (0.948)
  waiting for transfers between devices: 6.9 us -> 1.08 us
  Pallas kernels: 68.2 us -> 69.4 us
    ppermute x8, waiting for transfers between devices: 6.89 us -> 1.06 us  [swap(): return lax.ppermute(array, 'col', [(i, i ^ bit) for i in range(size)])]
    pallas_call x2 -> x3, Pallas kernels: 15.7 us -> 16.8 us  [the longest x2 16.6 us: load(): pl.pallas_call(kernel, name='load', in_specs=[ANY] * (count + len(after))...]
  transfers between devices with their start and end apart: 14 -> 14, of which waited for: 2 -> 2; matrix products, arithmetic and copies ran while one was open for 0% -> 0% of each run, Pallas kernels for 65% -> 70%
where the time goes in v1:
time: 87.3 us; the launch traced here: 87.1 us
  Pallas kernels  69.4 us (79%)
  starting transfers between devices  15 us (17%)
  waiting for transfers between devices  1.08 us (1%)
  between operations  0.91 us (1%)
    pallas_call x1, Pallas kernels, weight_grads(): pl.pallas_call(kernel, name='weight_grads', in_specs=[SMEM] * 3 + [VMEM]...  19 us
    pallas_call x2, Pallas kernels, load(): pl.pallas_call(kernel, name='load', in_specs=[ANY] * (count + len(after))...  16.6 us
    pallas_call x4, Pallas kernels, up_forward(): pl.pallas_call(kernel, name='up_forward', in_specs=[SMEM] + [VMEM] * (pie...  12.6 us
    pallas_call x2, Pallas kernels, input_part(): pl.pallas_call(kernel, name='input_part', in_specs=[SMEM] * 2 + [VMEM] *...  7.89 us
    pallas_call x2, Pallas kernels, output_part(): pl.pallas_call(kernel, name='output_part', in_specs=[SMEM] + [VMEM] * (pi...  7.14 us
    ppermute x3, starting transfers between devices, gather(): lax.ppermute(array, 'row', [(i, (i + s) % rows) for i in range(rows)])  6.11 us
    ppermute x8, starting transfers between devices, swap(): return lax.ppermute(array, 'col', [(i, i ^ bit) for i in range(size)])  4.75 us
    pallas_call x2, Pallas kernels, down_forward(): pl.pallas_call(kernel, name='down_forward', in_specs=[SMEM] + [VMEM] * (p...  4.67 us
  transfers between devices with their start and end apart: 14, of which 2 were waited for; matrix products, arithmetic and copies ran while one was open for 0% of the time, Pallas kernels for 70%

profile of v1, /device:TPU:0, one launch (start us, length us, event | category | flops | bytes accessed | tf_op | source)
XLA Modules:
  0.0 87.1 jit_solution(11273735296493281486)
XLA Ops:
  0.6 0.9 %join.1.rest_2_.rest_4_ = bf16[32,2048]{1,0:T(8,128)(2,1)S(1)} custom-call(bf16[16,2048]{1,0:T(8,128)(2,1)} %top_ref.1, bf16[16,2048]{1,0:T(8,128)(2,1)} %bottom_ref.1), custom_call_target="tpu_custom_call" | custom-call | tf_op jit(solution)/shard_map/join/pallas_call | solution.py:104
  1.5 5.1 %collective-permute-start.2 = (bf16[32,2048]{1,0:T(8,128)(2,1)S(1)}, bf16[32,2048]{1,0:T(8,128)(2,1)S(1)}, u32[]{:S(2)}, u32[]{:S(2)}) collective-permute-start(bf16[32,2048]{1,0:T(8,128)(2,1)S(1)} %join.1.rest_2_.rest_4_), channel_id=1, source_target_pairs={{0,12},{4,0},{8,4},{12,8},{1,13},{5,1},{9,5},{13,9},{2,14},{6,2},{... | collective-permute-start | bytes 393224 | tf_op jit(solution)/shard_map/ppermute | solution.py:527
  6.6 1.0 %collective-permute-start = (bf16[32,2048]{1,0:T(8,128)(2,1)S(1)}, bf16[32,2048]{1,0:T(8,128)(2,1)S(1)}, u32[]{:S(2)}, u32[]{:S(2)}) collective-permute-start(bf16[32,2048]{1,0:T(8,128)(2,1)S(1)} %join.1.rest_2_.rest_4_), channel_id=1, source_target_pairs={{0,4},{4,8},{8,12},{12,0},{1,5},{5,9},{9,13},{13,1},{2,6},{6,10},{... | collective-permute-start | bytes 393224 | tf_op jit(solution)/shard_map/ppermute | solution.py:527
  7.7 10.7 %load.2 = (bf16[1024,2048]{1,0:T(8,128)(2,1)S(1)}, bf16[1024,2048]{1,0:T(8,128)(2,1)S(1)}, bf16[1024,2048]{1,0:T(8,128)(2,1)S(1)}, bf16[1024,2048]{1,0:T(8,128)(...) custom-call(bf16[4096,2048]{1,0:T(8,128)(2,1)} %refs_0_.2, ...), custom_call_target="tpu_custom_call" | custom-call | bytes 33554432 | tf_op jit(solution)/shard_map/load/pallas_call | solution.py:138
  18.4 3.1 %up_forward.4.rest_6_ = bf16[64,2048]{1,0:T(8,128)(2,1)S(1)} custom-call(s32[16,32]{1,0:T(8,128)S(1)} %bitcast.2, bf16[1024,2048]{1,0:T(8,128)(2,1)S(1)} %get-tuple-element.24.rest_0_, bf16[1024,2048]{1,0:T(8,128)(2,1)S(1)} %get-tuple-element.25.rest_1_, bf16[32,2048]{1,0:T(8,128)(2,1)S(1)} %join.1.rest_2_.rest_4_, ...), custom_call_target="tpu_custom_call" | custom-call | flops 1 | bytes 1 | tf_op jit(solution)/shard_map/up_forward/pallas_call | solution.py:247
  21.6 0.1 collective-permute-start.3
  21.7 3.1 %up_forward.5.rest_7_ = bf16[64,2048]{1,0:T(8,128)(2,1)S(1)} custom-call(s32[16,32]{1,0:T(8,128)S(1)} %bitcast.7, bf16[1024,2048]{1,0:T(8,128)(2,1)S(1)} %get-tuple-element.26.rest_0_.rest_2_, bf16[1024,2048]{1,0:T(8,128)(2,1)S(1)} %get-tuple-element.27.rest_1_.rest_3_, bf16[32,2048]{1,0:T(8,128)(2,1)S(1)} %join.1.rest_2_.rest_4_, ...), custom_call_target="tpu_custom_call" | custom-call | flops 1 | bytes 1 | tf_op jit(solution)/shard_map/up_forward/pallas_call | solution.py:247
  24.8 0.5 collective-permute-start.5
  25.3 3.2 %up_forward.6.rest_7_.gate_ref = bf16[64,2048]{1,0:T(8,128)(2,1)S(1)} custom-call(s32[16,32]{1,0:T(8,128)S(1)} %bitcast.3, bf16[1024,2048]{1,0:T(8,128)(2,1)S(1)} %get-tuple-element.28.rest_0_, bf16[1024,2048]{1,0:T(8,128)(2,1)S(1)} %get-tuple-element.29.rest_1_, bf16[32,2048]{1,0:T(8,128)(2,1)S(1)} %join.1.rest_2_.rest_4_, ...), custom_call_target="tpu_custom_call" | custom-call | flops 1 | bytes 1 | tf_op jit(solution)/shard_map/up_forward/pallas_call | solution.py:247
  28.5 1.6 %collective-permute-start.4 = (bf16[64,2048]{1,0:T(8,128)(2,1)S(1)}, bf16[64,2048]{1,0:T(8,128)(2,1)S(1)}, u32[]{:S(2)}, u32[]{:S(2)}) collective-permute-start(bf16[64,2048]{1,0:T(8,128)(2,1)S(1)} %up_forward.6.rest_7_.gate_ref), channel_id=1, source_target_pairs={{0,2},{1,3},{2,0},{3,1},{4,6},{5,7},{6,4},{7,5},{8,10},{9,11},{10,... | collective-permute-start | bytes 786440 | tf_op jit(solution)/shard_map/ppermute | solution.py:533
  30.1 3.2 %up_forward.7.refs_1_.up_ref = bf16[64,2048]{1,0:T(8,128)(2,1)S(1)} custom-call(s32[16,32]{1,0:T(8,128)S(1)} %bitcast.8, bf16[1024,2048]{1,0:T(8,128)(2,1)S(1)} %get-tuple-element.30.rest_0_.rest_2_, bf16[1024,2048]{1,0:T(8,128)(2,1)S(1)} %get-tuple-element.31.rest_1_.rest_3_, bf16[32,2048]{1,0:T(8,128)(2,1)S(1)} %join.1.rest_2_.rest_4_, ...), custom_call_target="tpu_custom_call" | custom-call | flops 1 | bytes 1 | tf_op jit(solution)/shard_map/up_forward/pallas_call | solution.py:247
  33.3 0.6 collective-permute-start.6
  33.9 5.9 %load.3 = (bf16[2048,1024]{1,0:T(8,128)(2,1)S(1)}, bf16[2048,1024]{1,0:T(8,128)(2,1)S(1)}, bf16[2048,1024]{1,0:T(8,128)(2,1)S(1)}, bf16[2048,1024]{1,0:T(8,128)(2,1)S(1)}) custom-call(bf16[2048,4096]{1,0:T(8,128)(2,1)} %refs_0_.3, bf16[64,2048]{1,0:T(8,128)(2,1)S(1)} %up_forward.7.refs_1_.up_ref), custom_call_target="tpu_custom_call" | custom-call | flops 1 | bytes 1 | tf_op jit(solution)/shard_map/load/pallas_call | solution.py:138
  39.9 2.2 %down_forward.2.rest_0_ = bf16[64,2048]{1,0:T(8,128)(2,1)S(1)} custom-call(s32[16,32]{1,0:T(8,128)S(1)} %copy-done.4, bf16[2048,1024]{1,0:T(8,128)(2,1)S(1)} %get-tuple-element.34.rest_0_, bf16[2048,1024]{1,0:T(8,128)(2,1)S(1)} %get-tuple-element.35.rest_1_, bf16[32,2048]{1,0:T(8,128)(2,1)S(1)} %join.1.rest_2_.rest_4_, ...), custom_call_target="tpu_custom_call" | custom-call | flops 1 | bytes 1 | tf_op jit(solution)/shard_map/down_forward/pallas_call | solution.py:191
  42.1 0.1 collective-permute-start.7
  42.2 0.3 collective-permute-done.6.up_far_ref
  42.5 0.2 activate.1.rest_7_.rest_2_.rest_0_
  42.7 0.3 collective-permute-start.9
  42.9 0.8 collective-permute-done.7.rest_6_
  43.7 2.4 %down_forward.3.rest_3_.delta_ref = bf16[64,2048]{1,0:T(8,128)(2,1)S(1)} custom-call(s32[16,32]{1,0:T(8,128)S(1)} %copy-done.4, bf16[2048,1024]{1,0:T(8,128)(2,1)S(1)} %get-tuple-element.32.rest_0_, bf16[2048,1024]{1,0:T(8,128)(2,1)S(1)} %get-tuple-element.33.rest_1_, bf16[32,2048]{1,0:T(8,128)(2,1)S(1)} %join.1.rest_2_.rest_4_, ...), custom_call_target="tpu_custom_call" | custom-call | flops 1 | bytes 1 | tf_op jit(solution)/shard_map/down_forward/pallas_call | solution.py:191
  46.1 1.6 %collective-permute-start.8 = (bf16[64,2048]{1,0:T(8,128)(2,1)S(1)}, bf16[64,2048]{1,0:T(8,128)(2,1)S(1)}, u32[]{:S(2)}, u32[]{:S(2)}) collective-permute-start(bf16[64,2048]{1,0:T(8,128)(2,1)S(1)} %down_forward.3.rest_3_.delta_ref), channel_id=1, source_target_pairs={{0,2},{1,3},{2,0},{3,1},{4,6},{5,7},{6,4},{7,5},{8,10},{9,11},{10,... | collective-permute-start | bytes 786440 | tf_op jit(solution)/shard_map/ppermute | solution.py:533
  47.7 3.6 %output_part.2.rest_3_ = f32[64,2048]{1,0:T(8,128)S(1)} custom-call(s32[16,32]{1,0:T(8,128)S(1)} %copy-done.4, bf16[2048,1024]{1,0:T(8,128)(2,1)S(1)} %get-tuple-element.32.rest_0_, bf16[2048,1024]{1,0:T(8,128)(2,1)S(1)} %get-tuple-element.33.rest_1_, bf16[64,2048]{1,0:T(8,128)(2,1)S(1)} %activate.1.rest_7_.rest_2_.rest_0_, ...), custom_call_target="tpu_custom_call" | custom-call | flops 1 | bytes 1 | tf_op jit(solution)/shard_map/output_part/pallas_call | solution.py:345
  51.3 3.6 %output_part.3.rest_0_.rest_6_ = f32[64,2048]{1,0:T(8,128)S(1)} custom-call(s32[16,32]{1,0:T(8,128)S(1)} %copy-done.4, bf16[2048,1024]{1,0:T(8,128)(2,1)S(1)} %get-tuple-element.34.rest_0_, bf16[2048,1024]{1,0:T(8,128)(2,1)S(1)} %get-tuple-element.35.rest_1_, bf16[64,2048]{1,0:T(8,128)(2,1)S(1)} %collective-permute-done.9.rest_2_.rest_1_, ...), custom_call_target="tpu_custom_call" | custom-call | flops 1 | bytes 1 | tf_op jit(solution)/shard_map/output_part/pallas_call | solution.py:345
  54.9 0.4 deltas.1.rest_4_.rest_2_
  55.3 0.1 collective-permute-start.10
  55.3 3.9 %input_part.2.rest_5_ = f32[64,2048]{1,0:T(8,128)S(1)} custom-call(s32[16,32]{1,0:T(8,128)S(1)} %bitcast.4, s32[16,32]{1,0:T(8,128)S(1)} %bitcast.9, bf16[1024,2048]{1,0:T(8,128)(2,1)S(1)} %get-tuple-element.28.rest_0_, bf16[1024,2048]{1,0:T(8,128)(2,1)S(1)} %get-tuple-element.29.rest_1_, bf16[1024,2048]{1,0:T(8,128)(2,1)S(1)} %get-tuple-element.30.rest_0_.rest_2_, ...), custom_call_target="tpu_custom_call" | custom-call | flops 4294967296 | tf_op jit(solution)/shard_map/input_part/pallas_call | solution.py:408
  59.3 4.0 %input_part.3 = (bf16[32,2048]{1,0:T(8,128)(2,1)S(1)}, bf16[32,2048]{1,0:T(8,128)(2,1)S(1)}, bf16[32,2048]{1,0:T(8,128)(2,1)S(1)}, bf16[32,2048]{1,0:T(8,128)(2,1)S(1)}) custom-call(s32[16,32]{1,0:T(8,128)S(1)} %bitcast.5, s32[16,32]{1,0:T(8,128)S(1)} %bitcast.10, bf16[1024,2048]{1,0:T(8,128)(2,1)S(1)} %get-tuple-element.24.rest_0_, ...), custom_call_target="tpu_custom_call" | custom-call | flops 4294967296 | tf_op jit(solution)/shard_map/input_part/pallas_call | solution.py:408
  63.3 2.9 %collective-permute-start.11 = (bf16[32,2048]{1,0:T(8,128)(2,1)S(1)}, bf16[32,2048]{1,0:T(8,128)(2,1)S(1)}, u32[]{:S(2)}, u32[]{:S(2)}) collective-permute-start(bf16[32,2048]{1,0:T(8,128)(2,1)S(1)} %get-tuple-element.37), channel_id=1, source_target_pairs={{0,12},{4,0},{8,4},{12,8},{1,13},{5,1},{9,5},{13,9},{2,14},{6,2},{... | collective-permute-start | bytes 393224 | tf_op jit(solution)/shard_map/ppermute | solution.py:563
  66.1 1.1 %collective-permute-start.12 = (bf16[32,2048]{1,0:T(8,128)(2,1)S(1)}, bf16[32,2048]{1,0:T(8,128)(2,1)S(1)}, u32[]{:S(2)}, u32[]{:S(2)}) collective-permute-start(bf16[32,2048]{1,0:T(8,128)(2,1)S(1)} %get-tuple-element.38), channel_id=1, source_target_pairs={{0,8},{4,12},{8,0},{12,4},{1,9},{5,13},{9,1},{13,5},{2,10},{6,14},... | collective-permute-start | bytes 393224 | tf_op jit(solution)/shard_map/ppermute | solution.py:563
  67.2 0.1 collective-permute-start.13
  67.4 19.0 %weight_grads.1 = (bf16[4096,2048]{1,0:T(8,128)(2,1)}, bf16[4096,2048]{1,0:T(8,128)(2,1)}, bf16[2048,4096]{1,0:T(8,128)(2,1)}) custom-call(s32[16,32]{1,0:T(8,128)S(1)} %bitcast.6, s32[16,32]{1,0:T(8,128)S(1)} %bitcast.11, s32[16,32]{1,0:T(8,128)S(1)} %copy-done.4, bf16[64,2048]{1,0:T(8,128)(2,1)S(1)} %activate.1.rest_7_.rest_2_.rest_0_, ...), custom_call_target="tpu_custom_call" | custom-call | bytes 50331648 | tf_op jit(solution)/shard_map/weight_grads/pallas_call | solution.py:495
  86.5 0.7 fusion
  (24 shorter events, 0.1 us)
Async XLA Ops:
  1.5 16.9 %copy-start.2 = (s32[32,16]{0,1:T(8,128)S(1)}, s32[32,16]{0,1:T(8,128)}, u32[]{:S(2)}) copy-start(s32[32,16]{0,1:T(8,128)} %param.13) | copy-start | bytes 6148
  1.5 16.8 %collective-permute-start.2 = (bf16[32,2048]{1,0:T(8,128)(2,1)S(1)}, bf16[32,2048]{1,0:T(8,128)(2,1)S(1)}, u32[]{:S(2)}, u32[]{:S(2)}) collective-permute-start(bf16[32,2048]{1,0:T(8,128)(2,1)S(1)} %join.1.rest_2_.rest_4_), channel_id=1, source_target_pairs={{0,12},{4,0},{8,4},{12,8},{1,13},{5,1},{9,5},{13,9},{2,14},{6,2},{... | collective-permute-start | bytes 393224 | tf_op jit(solution)/shard_map/ppermute | solution.py:527
  6.6 11.7 %collective-permute-start.1 = (bf16[32,2048]{1,0:T(8,128)(2,1)S(1)}, bf16[32,2048]{1,0:T(8,128)(2,1)S(1)}, u32[]{:S(2)}, u32[]{:S(2)}) collective-permute-start(bf16[32,2048]{1,0:T(8,128)(2,1)S(1)} %join.1.rest_2_.rest_4_), channel_id=1, source_target_pairs={{0,8},{4,12},{8,0},{12,4},{1,9},{5,13},{9,1},{13,5},{2,10},{6,14},... | collective-permute-start | bytes 393224 | tf_op jit(solution)/shard_map/ppermute | solution.py:527
  6.6 11.8 %collective-permute-start = (bf16[32,2048]{1,0:T(8,128)(2,1)S(1)}, bf16[32,2048]{1,0:T(8,128)(2,1)S(1)}, u32[]{:S(2)}, u32[]{:S(2)}) collective-permute-start(bf16[32,2048]{1,0:T(8,128)(2,1)S(1)} %join.1.rest_2_.rest_4_), channel_id=1, source_target_pairs={{0,4},{4,8},{8,12},{12,0},{1,5},{5,9},{9,13},{13,1},{2,6},{6,10},{... | collective-permute-start | bytes 393224 | tf_op jit(solution)/shard_map/ppermute | solution.py:527
  18.4 3.3 %copy-start = (bf16[1024,2048]{1,0:T(8,128)(2,1)}, bf16[1024,2048]{1,0:T(8,128)(2,1)S(1)}, u32[]{:S(2)}) copy-start(bf16[1024,2048]{1,0:T(8,128)(2,1)S(1)} %get-tuple-element.26.rest_0_.rest_2_) | copy-start | bytes 12582916
  18.4 3.2 %copy-start.3 = (s32[32,16]{0,1:T(8,128)S(1)}, s32[32,16]{0,1:T(8,128)}, u32[]{:S(2)}) copy-start(s32[32,16]{0,1:T(8,128)} %param.14) | copy-start | bytes 6148
  21.6 3.8 %collective-permute-start.3 = (bf16[64,2048]{1,0:T(8,128)(2,1)S(1)}, bf16[64,2048]{1,0:T(8,128)(2,1)S(1)}, u32[]{:S(2)}, u32[]{:S(2)}) collective-permute-start(bf16[64,2048]{1,0:T(8,128)(2,1)S(1)} %up_forward.4.rest_6_), channel_id=1, source_target_pairs={{0,1},{1,0},{2,3},{3,2},{4,5},{5,4},{6,7},{7,6},{8,9},{9,8},{10,11... | collective-permute-start | bytes 786440 | tf_op jit(solution)/shard_map/ppermute | solution.py:533
  24.8 5.3 %collective-permute-start.5 = (bf16[64,2048]{1,0:T(8,128)(2,1)S(1)}, bf16[64,2048]{1,0:T(8,128)(2,1)S(1)}, u32[]{:S(2)}, u32[]{:S(2)}) collective-permute-start(bf16[64,2048]{1,0:T(8,128)(2,1)S(1)} %up_forward.5.rest_7_), channel_id=1, source_target_pairs={{0,1},{1,0},{2,3},{3,2},{4,5},{5,4},{6,7},{7,6},{8,9},{9,8},{10,11... | collective-permute-start | bytes 786440 | tf_op jit(solution)/shard_map/ppermute | solution.py:533
  28.5 11.3 %collective-permute-start.4 = (bf16[64,2048]{1,0:T(8,128)(2,1)S(1)}, bf16[64,2048]{1,0:T(8,128)(2,1)S(1)}, u32[]{:S(2)}, u32[]{:S(2)}) collective-permute-start(bf16[64,2048]{1,0:T(8,128)(2,1)S(1)} %up_forward.6.rest_7_.gate_ref), channel_id=1, source_target_pairs={{0,2},{1,3},{2,0},{3,1},{4,6},{5,7},{6,4},{7,5},{8,10},{9,11},{10,... | collective-permute-start | bytes 786440 | tf_op jit(solution)/shard_map/ppermute | solution.py:533
  33.3 6.6 %copy-start.4 = (s32[16,32]{1,0:T(8,128)S(1)}, s32[16,32]{1,0:T(8,128)}, u32[]{:S(2)}) copy-start(s32[16,32]{1,0:T(8,128)} %down_mask_ref.1) | copy-start | bytes 6148
  33.3 9.2 %collective-permute-start.6 = (bf16[64,2048]{1,0:T(8,128)(2,1)S(1)}, bf16[64,2048]{1,0:T(8,128)(2,1)S(1)}, u32[]{:S(2)}, u32[]{:S(2)}) collective-permute-start(bf16[64,2048]{1,0:T(8,128)(2,1)S(1)} %up_forward.7.refs_1_.up_ref), channel_id=1, source_target_pairs={{0,2},{1,3},{2,0},{3,1},{4,6},{5,7},{6,4},{7,5},{8,10},{9,11},{10,... | collective-permute-start | bytes 786440 | tf_op jit(solution)/shard_map/ppermute | solution.py:533
  42.1 1.6 %collective-permute-start.7 = (bf16[64,2048]{1,0:T(8,128)(2,1)S(1)}, bf16[64,2048]{1,0:T(8,128)(2,1)S(1)}, u32[]{:S(2)}, u32[]{:S(2)}) collective-permute-start(bf16[64,2048]{1,0:T(8,128)(2,1)S(1)} %down_forward.2.rest_0_), channel_id=1, source_target_pairs={{0,1},{1,0},{2,3},{3,2},{4,5},{5,4},{6,7},{7,6},{8,9},{9,8},{10,11... | collective-permute-start | bytes 786440 | tf_op jit(solution)/shard_map/ppermute | solution.py:533
  42.7 8.6 %collective-permute-start.9 = (bf16[64,2048]{1,0:T(8,128)(2,1)S(1)}, bf16[64,2048]{1,0:T(8,128)(2,1)S(1)}, u32[]{:S(2)}, u32[]{:S(2)}) collective-permute-start(bf16[64,2048]{1,0:T(8,128)(2,1)S(1)} %activate.1.rest_7_.rest_2_.rest_0_), channel_id=1, source_target_pairs={{0,1},{1,0},{2,3},{3,2},{4,5},{5,4},{6,7},{7,6},{8,9},{9,8},{10,11... | collective-permute-start | bytes 786440 | tf_op jit(solution)/shard_map/ppermute | solution.py:533
  46.1 8.7 %collective-permute-start.8 = (bf16[64,2048]{1,0:T(8,128)(2,1)S(1)}, bf16[64,2048]{1,0:T(8,128)(2,1)S(1)}, u32[]{:S(2)}, u32[]{:S(2)}) collective-permute-start(bf16[64,2048]{1,0:T(8,128)(2,1)S(1)} %down_forward.3.rest_3_.delta_ref), channel_id=1, source_target_pairs={{0,2},{1,3},{2,0},{3,1},{4,6},{5,7},{6,4},{7,5},{8,10},{9,11},{10,... | collective-permute-start | bytes 786440 | tf_op jit(solution)/shard_map/ppermute | solution.py:533
  55.2 4.0 %copy-start.1 = (bf16[1024,2048]{1,0:T(8,128)(2,1)S(1)}, bf16[1024,2048]{1,0:T(8,128)(2,1)}, u32[]{:S(2)}) copy-start(bf16[1024,2048]{1,0:T(8,128)(2,1)} %copy-done) | copy-start | bytes 12582916
  55.3 4.0 %collective-permute-start.10 = (bf16[128,2048]{1,0:T(8,128)(2,1)S(1)}, bf16[128,2048]{1,0:T(8,128)(2,1)S(1)}, u32[]{:S(2)}, u32[]{:S(2)}) collective-permute-start(bf16[128,2048]{1,0:T(8,128)(2,1)S(1)} %deltas.1.rest_4_.rest_2_), channel_id=1, source_target_pairs={{0,1},{1,0},{2,3},{3,2},{4,5},{5,4},{6,7},{7,6},{8,9},{9,8},{10,11... | collective-permute-start | bytes 1572872 | tf_op jit(solution)/shard_map/ppermute | solution.py:533
  63.3 23.1 %collective-permute-start.11 = (bf16[32,2048]{1,0:T(8,128)(2,1)S(1)}, bf16[32,2048]{1,0:T(8,128)(2,1)S(1)}, u32[]{:S(2)}, u32[]{:S(2)}) collective-permute-start(bf16[32,2048]{1,0:T(8,128)(2,1)S(1)} %get-tuple-element.37), channel_id=1, source_target_pairs={{0,12},{4,0},{8,4},{12,8},{1,13},{5,1},{9,5},{13,9},{2,14},{6,2},{... | collective-permute-start | bytes 393224 | tf_op jit(solution)/shard_map/ppermute | solution.py:563
  66.1 20.3 %collective-permute-start.12 = (bf16[32,2048]{1,0:T(8,128)(2,1)S(1)}, bf16[32,2048]{1,0:T(8,128)(2,1)S(1)}, u32[]{:S(2)}, u32[]{:S(2)}) collective-permute-start(bf16[32,2048]{1,0:T(8,128)(2,1)S(1)} %get-tuple-element.38), channel_id=1, source_target_pairs={{0,8},{4,12},{8,0},{12,4},{1,9},{5,13},{9,1},{13,5},{2,10},{6,14},... | collective-permute-start | bytes 393224 | tf_op jit(solution)/shard_map/ppermute | solution.py:563
  67.2 19.2 %collective-permute-start.13 = (bf16[32,2048]{1,0:T(8,128)(2,1)S(1)}, bf16[32,2048]{1,0:T(8,128)(2,1)S(1)}, u32[]{:S(2)}, u32[]{:S(2)}) collective-permute-start(bf16[32,2048]{1,0:T(8,128)(2,1)S(1)} %get-tuple-element.39), channel_id=1, source_target_pairs={{0,4},{4,8},{8,12},{12,0},{1,5},{5,9},{9,13},{13,1},{2,6},{6,10},{... | collective-permute-start | bytes 393224 | tf_op jit(solution)/shard_map/ppermute | solution.py:563
